TPU v7x, 256 devices: a whole 4x4x8 slice. The times are simulated.
256 devices in a mesh: group: 16 (over y, z_hi, core), dev: 16 (over z_lo, x).
Axes of the slice: x: 4, y: 4, z: 8 (z_hi: 2, z_lo: 4; z = z_hi * 4 + z_lo), core: 2. Of those that a mesh axis runs over, the one named last changes fastest.
Arguments:
- question_encoder_states: bfloat16 [2048, 1024], P(('group', 'dev')), may hold values from -24 to 24
- query_proj: bfloat16 [1024, 768], replicated, may hold values from -0.1875 to 0.1875
- positive_embed: bfloat16 [2048, 768], P(('group', 'dev')), may hold values from -6 to 6
- stale_index: bfloat16 [524288, 768], P(('group', 'dev')), may hold values from -6 to 6
- neg_owner: int32 [2048, 128, 1], P(('group', 'dev')), may hold values from 0 to 255; in each aligned block of 1024 rows (0 to 1023, 1024 to 2047, ..., all dimensions but the last counted through in order) at most 8 rows name the same one
- neg_row: int32 [2048, 128], P(('group', 'dev')), may hold values from 0 to 2047
- neg_count: int32 [2048], P(('group', 'dev')), may hold values from 1 to 128, 196608 in all
- slab_hidden: bfloat16 [524288, 1024], P(('group', 'dev')), may hold values from -6 to 6
- passage_projector: bfloat16 [1024, 768], P(None, 'dev'), may hold values from -0.1875 to 0.1875
Outputs:
- losses: float32 [2048], P(('group', 'dev'))
- proj_grad: float32 [1024, 768], P('dev')
- renewed_document_vectors: bfloat16 [524288, 768], P(('group', 'dev'))
Inputs may be any that keep to these rules, and one draw needn't show every extreme that they name: `neg_owner`: among the 128 slots of the 8 queries of one device, no shard is named more than 8 times.
All inputs are finite; a program needn't handle non-finite values. No bound on the sum of `neg_count` on one device may be relied on, other than what follows from the above.
Results may differ from a plain program's by a relative error of at most 0.001.
Values may be sent and summed in bfloat16 or wider, within the bound.
A program may use at most 64 MiB of HBM per device.

v0:
```python
import jax
import jax.numpy as jnp
from jax import lax
from jax.sharding import PartitionSpec as P

epsilon = 1e-06
sharpness_divisor = 0.05


def normalized_rows(values):
    return values * lax.rsqrt(jnp.mean(values * values, axis=-1, keepdims=True) + epsilon)


def query_loss(question_vector_raw_length, positive_passage, fetched, live_count):
    query_unit = normalized_rows(question_vector_raw_length)
    pos_unit = normalized_rows(positive_passage.astype(jnp.float32))
    neg_unit = normalized_rows(fetched.astype(jnp.float32))
    similarity_multiplier = 1.0 / (question_vector_raw_length.shape[-1] * sharpness_divisor)
    pos_score = jnp.sum(query_unit * pos_unit, axis=-1) * similarity_multiplier
    neg_score = (
        jnp.einsum("be,bne->bn", query_unit, neg_unit, precision=lax.Precision.HIGHEST)
        * similarity_multiplier
    )
    candidate_position_range = lax.broadcasted_iota(jnp.int32, neg_score.shape, 1)
    live_mask = candidate_position_range < live_count[:, None]
    partition = jnp.exp(pos_score) + jnp.sum(jnp.where(live_mask, jnp.exp(neg_score), 0.0), axis=-1)
    return jnp.log(partition) - pos_score


def local(
    question_encoder_states,
    query_proj,
    positive_embed,
    stale_index,
    neg_owner,
    neg_row,
    neg_count,
    slab_hidden,
    passage_projector,
):
    group_count = lax.axis_size("group")
    accelerator_number = lax.axis_size("dev")
    owner_count = group_count * accelerator_number
    row_width = stale_index.shape[1]
    queries_here = neg_row.shape[0]
    slots_per_query = neg_row.shape[1]
    rows_here = queries_here * slots_per_query
    capacity = max(2, 2 * rows_here // owner_count)
    owner_flat = neg_owner.reshape(rows_here)
    flattened_rows = neg_row.reshape(rows_here)
    owner_hits = (
        owner_flat[:, None] == lax.broadcasted_iota(jnp.int32, (1, owner_count), 1)
    ).astype(jnp.int32)
    slot_rank = jnp.sum((jnp.cumsum(owner_hits, axis=0) - 1) * owner_hits, axis=1)
    slot_index = owner_flat * capacity + slot_rank
    requests = jnp.zeros((owner_count * capacity,), jnp.int32).at[slot_index].set(flattened_rows)
    requests = requests.reshape(group_count, accelerator_number, capacity)
    asked = lax.all_to_all(
        lax.all_to_all(requests, "group", split_axis=0, concat_axis=0, tiled=True),
        "dev",
        split_axis=1,
        concat_axis=1,
        tiled=True,
    )
    picked = jnp.take(stale_index, asked.reshape(-1), axis=0).reshape(asked.shape + (row_width,))
    answered = lax.all_to_all(picked, "dev", split_axis=1, concat_axis=1, tiled=True)
    arrived = lax.all_to_all(answered, "group", split_axis=0, concat_axis=0, tiled=True)
    fetched = arrived.reshape(owner_count * capacity, row_width)[slot_index]
    fetched = fetched.reshape(queries_here, slots_per_query, row_width)
    question_vector_raw_length = jnp.dot(
        question_encoder_states, query_proj, preferred_element_type=jnp.float32
    )
    losses, backward_pass = jax.vjp(
        lambda query_vec: query_loss(query_vec, positive_embed, fetched, neg_count),
        question_vector_raw_length,
    )
    (pull_back,) = backward_pass(jnp.ones_like(losses))
    feature_count = question_encoder_states.shape[1]
    row_share = feature_count // accelerator_number
    wide_hidden = question_encoder_states.astype(jnp.float32)
    grad_term = jnp.dot(wide_hidden.T, pull_back, precision=lax.Precision.HIGHEST)
    summed = lax.psum(grad_term, ("group", "dev"))
    proj_grad = lax.dynamic_slice_in_dim(summed, lax.axis_index("dev") * row_share, row_share, 0)
    renewed_document_vectors = jnp.dot(
        slab_hidden,
        lax.all_gather(passage_projector, "dev", axis=1, tiled=True),
        preferred_element_type=jnp.float32,
    ).astype(jnp.bfloat16)
    return (losses, proj_grad, renewed_document_vectors)


def solution(mesh):
    in_specs = (
        P(("group", "dev"), None),
        P(),
        P(("group", "dev"), None),
        P(("group", "dev"), None),
        P(("group", "dev"), None, None),
        P(("group", "dev"), None),
        P(("group", "dev")),
        P(("group", "dev"), None),
        P(None, "dev"),
    )
    out_specs = (P(("group", "dev")), P("dev", None), P(("group", "dev"), None))
    return jax.shard_map(local, mesh=mesh, in_specs=in_specs, out_specs=out_specs, check_vma=False)
```

profile of v0, /device:TPU:1, one launch (start us, length us, event | category | flops | bytes accessed | tf_op | source)
XLA Modules:
  0.0 522.9 jit_solution(7200198531816201405)
XLA Ops:
  8.0 0.9 copy.35
  9.0 0.2 fusion.7
  9.2 1.0 copy-done.2
  10.2 1.3 add_add_fusion
  11.5 0.3 copy.36
  11.8 0.4 fusion.6
  12.2 4.5 scatter_custom_fusion
  17.0 21.8 %all_to_all.20 = s32[16,1,128]{2,1,0:T(1,128)S(1)} all-to-all(s32[16,1,128]{2,1,0:T(1,128)S(1)} %reshape.187), channel_id=1, replica_groups=mesh['group'=16,'dev'=16] {'group'}, dimensions={0} | all-to-all | bytes 16384 | tf_op jit(solution)/shard_map/all_to_all | solution.py:59
  38.8 0.5 broadcast.212
  39.3 0.7 reduce.1
  40.3 12.1 %all_to_all.21 = s32[16,1,128]{2,1,0:T(1,128)S(1)} all-to-all(s32[16,1,128]{2,1,0:T(1,128)S(1)} %reshape.189), channel_id=1, replica_groups=mesh['group'=16,'dev'=16] {'dev'}, dimensions={0} | all-to-all | bytes 16384 | tf_op jit(solution)/shard_map/all_to_all | solution.py:58
  52.3 0.7 reduce.2
  53.5 9.4 %gather_fusion = bf16[2048,768]{1,0:T(8,128)(2,1)} fusion(bf16[2048,768]{1,0:T(8,128)(2,1)S(1)} %copy-done, s32[2048]{0:T(1024)S(1)} %broadcast_clamp_fusion), kind=kCustom, calls=%fused_computation | custom fusion | bytes 6299648 | tf_op jit(solution)/shard_map/jit(_take)/gather | solution.py:65
  62.9 2.1 copy_select_fusion
  65.1 72.2 %all_to_all.22 = bf16[16,16,8,768]{3,2,0,1:T(8,128)(2,1)S(1)} all-to-all(bf16[16,16,8,768]{3,2,0,1:T(8,128)(2,1)S(1)} %copy_select_fusion), channel_id=1, replica_groups=mesh['group'=16,'dev'=16] {'dev'}, dimensions={1} | all-to-all | bytes 6291456 | tf_op jit(solution)/shard_map/all_to_all | solution.py:66
  137.3 2.0 copy.42
  139.3 7.4 %all-to-all-start.3 = ((bf16[16,16,8,768]{3,2,1,0:T(8,128)(2,1)}), bf16[16,16,8,768]{3,2,1,0:T(8,128)(2,1)}, u32[]{:S(2)}, u32[]{:S(2)}) async-start(bf16[16,16,8,768]{3,2,1,0:T(8,128)(2,1)} %copy.42), calls=%async_computation.3 | async-start | bytes 6291456 | tf_op jit(solution)/shard_map/all_to_all | solution.py:67
  146.7 0.7 all-gather.2.cloned.1.call-update
  147.4 0.2 all-reduce.2.cloned.1.call-start
  147.6 1.8 multiply_reduce_fusion.2
  149.8 59.2 %all-to-all-done.3 = bf16[16,16,8,768]{3,2,1,0:T(8,128)(2,1)} async-done(((bf16[16,16,8,768]{3,2,1,0:T(8,128)(2,1)}), bf16[16,16,8,768]{3,2,1,0:T(8,128)(2,1)}, u32[]{:S(2)}, u32[]{:S(2)}) %all-to-all-start.3) | async-done | bytes 3145760 | tf_op jit(solution)/shard_map/all_to_all | solution.py:67
  209.1 7.9 %gather_fusion.1 = bf16[1024,768]{1,0:T(8,128)(2,1)} fusion(bf16[2048,768]{1,0:T(8,128)(2,1)} %bitcast.12, s32[1024]{0:T(1024)S(1)} %broadcast_clamp_fusion.1), kind=kCustom, calls=%fused_computation.1 | custom fusion | bytes 3149824 | tf_op jit(solution)/shard_map/gather | solution.py:68
  216.9 1.9 multiply_reduce_fusion
  218.9 4.1 fusion.2
  223.2 0.5 add_multiply_fusion
  223.8 1.8 fusion
  225.8 3.2 convolution_bitcast_fusion
  229.1 13.4 %all-gather.2.cloned.1.call-done = bf16[1024,768]{0,1:T(8,128)(2,1)} async-done(((bf16[1024,48]{0,1:T(8,128)(2,1)}), bf16[1024,768]{0,1:T(8,128)(2,1)}) %all-gather.2.cloned.1.call-update) | async-done | bytes 1572880 | tf_op jit(solution)/shard_map/all_gather | solution.py:86
  242.5 7.8 %convolution_convert_fusion = bf16[2048,768]{1,0:T(8,128)(2,1)} fusion(bf16[2048,1024]{1,0:T(8,128)(2,1)} %param.16, bf16[1024,768]{0,1:T(8,128)(2,1)} %all-gather.2.cloned.1.call-done), kind=kOutput, calls=%fused_computation.3 | convolution fusion | flops 3222798336 | bytes 8912896 | tf_op jit(solution)/shard_map/dot_general | solution.py:84
  250.3 263.1 %all-reduce.2.cloned.1.call-done = f32[1024,768]{0,1:T(8,128)} async-done(((f32[1024,768]{0,1:T(8,128)}), f32[1024,768]{0,1:T(8,128)}) %all-reduce.2.cloned.1.call-update) | async-done | bytes 3145744 | tf_op jit(solution)/shard_map/psum | solution.py:82
  513.4 1.2 constant_dynamic-slice_fusion
  514.6 0.8 copy.43
  (41 shorter events, 1.9 us)
Async XLA Ops:
  8.0 45.5 %copy-start = (bf16[2048,768]{1,0:T(8,128)(2,1)S(1)}, bf16[2048,768]{1,0:T(8,128)(2,1)}, u32[]{:S(2)}) copy-start(bf16[2048,768]{1,0:T(8,128)(2,1)} %param.12) | copy-start | bytes 9437188
  8.0 3.8 copy-start.5
  9.2 1.0 copy-start.2
  139.3 8.3 %copy-start.4 = (bf16[8,1024]{1,0:T(8,128)(2,1)S(1)}, bf16[8,1024]{1,0:T(8,128)(2,1)}, u32[]{:S(2)}) copy-start(bf16[8,1024]{1,0:T(8,128)(2,1)} %param.9) | copy-start | bytes 49156
  139.3 10.2 %copy-start.3 = (bf16[8,768]{1,0:T(8,128)(2,1)S(1)}, bf16[8,768]{1,0:T(8,128)(2,1)}, u32[]{:S(2)}) copy-start(bf16[8,768]{1,0:T(8,128)(2,1)} %param.11) | copy-start | bytes 36868
  139.3 69.8 %all-to-all-start.3 = ((bf16[16,16,8,768]{3,2,1,0:T(8,128)(2,1)}), bf16[16,16,8,768]{3,2,1,0:T(8,128)(2,1)}, u32[]{:S(2)}, u32[]{:S(2)}) async-start(bf16[16,16,8,768]{3,2,1,0:T(8,128)(2,1)} %copy.42), calls=%async_computation.3 | async-start | bytes 6291456 | tf_op jit(solution)/shard_map/all_to_all | solution.py:67
  146.7 95.8 %all-gather.2.cloned.1.call-start = ((), (), s32[]{:S(2)}) async-start(), calls=%async_computation.5 | async-start | bytes 1671168 | tf_op jit(solution)/shard_map/all_gather | solution.py:86
  147.4 366.0 %all-reduce.2.cloned.1.call-start = ((), (), s32[]{:S(2)}) async-start(), calls=%async_computation.4 | async-start | bytes 6291456 | tf_op jit(solution)/shard_map/psum | solution.py:82
  216.9 6.0 %copy-start.6 = (s32[8]{0:T(128)S(1)}, s32[8]{0:T(128)}, u32[]{:S(2)}) copy-start(s32[8]{0:T(128)} %param.15) | copy-start | bytes 100
  216.9 6.8 %copy-start.1 = (bf16[1024,768]{1,0:T(8,128)(2,1)S(1)}, bf16[1024,768]{1,0:T(8,128)(2,1)}, u32[]{:S(2)}) copy-start(bf16[1024,768]{1,0:T(8,128)(2,1)} %gather_fusion.1) | copy-start | bytes 4718596
Sparse Core Ops, SparseCore 0:
  149.4 93.0 all-gather.1
Sparse Core Ops, SparseCore 1:
  229.1 284.2 all-reduce.1
where the time goes:
time: 524 us; the launch traced here: 523 us
  waiting for transfers between devices  336 us (64%)
  blocking collectives  106 us (20%)
  local copies, waits for them, and re-layouts  29.5 us (6%)
  matrix products  18.8 us (4%)
  between operations  15.7 us (3%)
  other arithmetic  8.64 us (2%)
  starting transfers between devices  7.63 us (1%)
    psum x1, waiting for transfers between devices, local(): summed = lax.psum(grad_term, ('group', 'dev'))  263 us
    all_to_all x1, blocking collectives, local(): lax.all_to_all(picked, 'dev', split_axis=1, concat_axis=1, tiled=True)  72.2 us
    all_to_all x1, waiting for transfers between devices, local(): lax.all_to_all(answered, 'group', split_axis=0, concat_axis=0, tiled=True)  59.2 us
    all_to_all x1, blocking collectives, local(): lax.all_to_all(requests, 'group', split_axis=0, concat_axis=0, tiled=True)  21.8 us
    all_gather x1, waiting for transfers between devices, local(): lax.all_gather(passage_projector, 'dev', axis=1, tiled=True)  13.4 us
    all_to_all x1, blocking collectives, local(): lax.all_to_all(lax.all_to_all(requests, 'group', split_axis=0, concat_axi...  12.1 us
  transfers between devices with their start and end apart: 3, of which 3 were waited for; matrix products, arithmetic and copies ran while one was open for 6% of the time, Pallas kernels for 0%

commit v1 on v0

v1 whole, which is shorter than its diff:
```python
import jax
import jax.numpy as jnp
from jax import lax
from jax.experimental import pallas as pl
from jax.experimental.pallas import tpu as pltpu
from jax.sharding import PartitionSpec as P

MESH = pl.DeviceIdType.MESH
F32 = jnp.float32
BF16 = jnp.bfloat16
EPS = 1e-06
DIV = 0.05
E = 768
D = 1024
SCALE = 1.0 / (E * DIV)
NX, NY, NZ = 4, 4, 8
X_FIRST = (True, True, False, True, False, False)


def iota(shape, dim):
    return lax.broadcasted_iota(jnp.int32, shape, dim)


def nt(a, b):
    return lax.dot_general(a, b, (((1,), (1,)), ((), ())), preferred_element_type=F32)


def tn(a, b):
    return lax.dot_general(a, b, (((0,), (0,)), ((), ())), preferred_element_type=F32)


def device_of(x, y, z, c):
    return ((y * 2 + z // 4) * 2 + c, lax.rem(z, 4) * 4 + x)


def body(
    h_ref, req_ref, pos_ref, pt_ref, wq_hbm, idx_hbm, slab_hbm,
    loss_ref, grad_ref, ren_hbm,
    wq, idx, slab, ren, local_sem,
    buf_a, buf_b, h_t, tab, tab_z, tab_y, tab_j, tab_r,
    pbuf, rows, ghat, gmat, zbuf, zrecv, zsum, zcol,
    tt, tcore, tsum, r1, p1, r2, p2, r3, fin,
    ssem, rsem,
):
    g = lax.axis_index("group")
    d = lax.axis_index("dev")
    x = lax.rem(d, 4)
    c = lax.rem(g, 2)
    y = g // 4
    z = lax.rem(g // 2, 2) * 4 + d // 4
    blk = x * 2 + c

    def near(dx, dy, dz, dc):
        return (
            lax.rem(x + dx + NX, NX),
            lax.rem(y + dy + NY, NY),
            lax.rem(z + dz + NZ, NZ),
            lax.rem(c + dc, 2),
        )

    used = [0]
    sent = []

    def copy(src, dst, at):
        n = used[0]
        used[0] = n + 1
        r = pltpu.make_async_remote_copy(
            src_ref=src, dst_ref=dst, send_sem=ssem.at[n], recv_sem=rsem.at[n],
            device_id=device_of(*at), device_id_type=MESH,
        )
        r.start()
        sent.append(r)
        return r

    loads = []
    for n, (src, dst) in enumerate(((wq_hbm, wq), (idx_hbm, idx), (slab_hbm, slab))):
        load = pltpu.make_async_copy(src, dst, local_sem.at[n])
        load.start()
        loads.append(load)

    peers = [(0, 0, i, 0) for i in range(1, NZ)]
    peers += [(i, j, 0, 0) for i in range(NX) for j in range(NY) if i or j]
    peers += [(i, 0, 0, 1) for i in range(NX)]
    peers += [(0, j, 0, 1) for j in range(1, NY)]
    barrier = pltpu.get_barrier_semaphore()
    for p in peers:
        pl.semaphore_signal(barrier, inc=1, device_id=device_of(*near(*p)), device_id_type=MESH)

    h32 = h_ref[...].astype(F32)
    buf_a[x, c, y, z] = jnp.concatenate([h32[:, 0:256], h32[:, 256:512]], axis=0).astype(BF16)
    buf_b[x, c, y, z] = jnp.concatenate([h32[:, 512:768], h32[:, 768:1024]], axis=0).astype(BF16)
    pbuf[c, lax.rem(z, 4), x] = pt_ref[c]
    pl.semaphore_wait(barrier, len(peers))

    z_a = [copy(buf_a.at[x, c, y, z], buf_a.at[x, c, y, z], near(0, 0, o, 0)) for o in range(1, NZ)]
    z_b = [copy(buf_b.at[x, c, y, z], buf_b.at[x, c, y, z], near(0, 0, o, 0)) for o in range(1, NZ)]
    zl = lax.rem(z, 4)
    p_x = [copy(pbuf.at[c, zl, x], pbuf.at[c, zl, x], near(o, 0, 0, 0)) for o in range(1, NX)]

    lane = iota((128, 128), 1)
    kind, place = lane % 16, lane // 16
    lower = (iota((128, 128), 0) > lane).astype(F32).astype(BF16)
    owner_lane = iota((128, 256), 1).astype(F32)
    carry = jnp.zeros((1, 256), F32)
    table = jnp.zeros((256, 128), F32)
    for i in range(8):
        code = req_ref[:, i:i + 1]
        row = req_ref[:, 8 + i:9 + i]
        hit = (code == owner_lane).astype(F32)
        before = jnp.dot(lower, hit.astype(BF16), preferred_element_type=F32) + carry
        rank = jnp.sum(hit * before, axis=1, keepdims=True)
        carry = carry + jnp.sum(hit, axis=0, keepdims=True)
        high = jnp.floor(row * (1.0 / 16.0))
        low = row - 16.0 * high
        value = jnp.where(kind == 0, high, jnp.where(kind == 1, low, jnp.where(kind == 2, i + 1.0, 0.0)))
        value = jnp.where(rank == place.astype(F32), value, 0.0)
        table = table + tn(hit.astype(BF16), value.astype(BF16))
    tab[...] = table.reshape(NZ, NY, 8, 128)

    t_z = [
        copy(tab.at[near(0, 0, o, 0)[2]], tab_z.at[z], near(0, 0, o, 0)) for o in range(1, NZ)
    ]
    tab_z[z] = tab[z]

    def spread(buf, waits, mid, last):
        for w in waits:
            w.wait_recv()
        mids = [copy(buf.at[x, c, y], buf.at[x, c, y], near(*mid(o))) for o in range(1, 4)]
        lasts = [copy(buf.at[x, c, y], buf.at[x, c, y], near(*last(o))) for o in range(1, 4)]
        cores = [copy(buf.at[x, c, y], buf.at[x, c, y], near(0, 0, 0, 1))]
        return mids, lasts, cores

    def along_x(o):
        return (o, 0, 0, 0)

    def along_y(o):
        return (0, o, 0, 0)

    mid_a, last_a, core_a = spread(buf_a, z_a, along_y, along_x)
    mid_b, last_b, core_b = spread(buf_b, z_b, along_x, along_y)

    for w in t_z:
        w.wait_recv()
    t_y = [
        copy(tab_z.at[:, near(0, o, 0, 0)[1]], tab_y.at[y], near(0, o, 0, 0)) for o in range(1, NY)
    ]
    tab_y[y] = tab_z[:, y]

    for w in p_x:
        w.wait_recv()
    p_z = [copy(pbuf.at[c, zl], pbuf.at[c, zl], near(0, 0, o, 0)) for o in (1, 7)]
    p_z += [copy(pbuf.at[c, zl, 0:2], pbuf.at[c, zl, 0:2], near(0, 0, 2, 0))]
    p_z += [copy(pbuf.at[c, zl, 2:4], pbuf.at[c, zl, 2:4], near(0, 0, 6, 0))]

    for o in range(1, 4):
        mid_a[o - 1].wait_recv()
        grp = buf_a.at[x, c, lax.rem(y - o + NY, NY)]
        last_a += [copy(grp, grp, near(*along_x(q))) for q in range(1, 4)]
        core_a.append(copy(grp, grp, near(0, 0, 0, 1)))
        mid_b[o - 1].wait_recv()
        grp = buf_b.at[lax.rem(x - o + NX, NX), c, y]
        last_b += [copy(grp, grp, near(*along_y(q))) for q in range(1, 4)]
        core_b.append(copy(grp, grp, near(0, 0, 0, 1)))

    for w in t_y:
        w.wait_recv()
    tab_j[...] = jnp.swapaxes(tab_y[...].reshape(NY * NZ, 8, 128), 0, 1)
    t_j = []
    for o in range(NX):
        for k in range(2):
            if o or k:
                at = near(o, 0, 0, k)
                t_j.append(copy(tab_j.at[at[0] * 2 + at[3]], tab_r.at[blk], at))
    tab_r[blk] = tab_j[blk]

    loads[0].wait()
    q_own = jnp.dot(h_ref[...], wq[...], preferred_element_type=F32)
    rq_own = lax.rsqrt(jnp.mean(q_own * q_own, axis=1, keepdims=True) + EPS)
    u_own = q_own * rq_own
    pos = pos_ref[...].astype(F32)
    pos = pos * lax.rsqrt(jnp.mean(pos * pos, axis=1, keepdims=True) + EPS)
    pos_dot = jnp.sum(u_own * pos, axis=1, keepdims=True)
    pos_score = pos_dot * SCALE
    pos_exp = jnp.exp(pos_score)
    pos_dir = (pos - u_own * (pos_dot * (1.0 / E))) * (rq_own * SCALE)

    loads[1].wait()
    for w in t_j:
        w.wait_recv()
    src, out = iota((128, 2048), 0), iota((128, 2048), 1)
    slot, want_q = out // 256, (out // 128) % 2
    weight = jnp.where(src % 16 == 0, 16.0, 1.0)
    kept = jnp.where(want_q == 0, jnp.where(src % 16 < 2, weight, 0.0), jnp.where(src % 16 == 2, 1.0, 0.0))
    expand = jnp.where(src // 16 == slot, kept, 0.0).astype(BF16)

    def columns_of(b):
        wide = jnp.dot(tab_r[b].astype(BF16), expand, preferred_element_type=F32)
        row = jnp.concatenate([wide[:, k * 256:k * 256 + 128] for k in range(8)], axis=0)
        qry = jnp.concatenate([wide[:, k * 256 + 128:k * 256 + 256] for k in range(8)], axis=0)
        return row, qry

    lane_f = iota((256, 128), 1).astype(F32)

    def pick(b, _):
        row, _q = columns_of(b)
        hot = jnp.concatenate(
            [(row == lane_f + 128.0 * t).astype(F32).astype(BF16) for t in range(16)], axis=1
        )
        rows[b] = jnp.dot(hot, idx[...], preferred_element_type=F32).astype(BF16)
        return 0

    lax.fori_loop(0, 8, pick, 0)

    for j in range(4):
        for q in range(1, 4):
            last_a[j * 3 + q - 1].wait_recv()
            grp = buf_a.at[lax.rem(x - q + NX, NX), c, lax.rem(y - j + NY, NY)]
            core_a.append(copy(grp, grp, near(0, 0, 0, 1)))
            last_b[j * 3 + q - 1].wait_recv()
            grp = buf_b.at[lax.rem(x - j + NX, NX), c, lax.rem(y - q + NY, NY)]
            core_b.append(copy(grp, grp, near(0, 0, 0, 1)))
    for w in p_z:
        w.wait_recv()
    p_c = copy(pbuf.at[c], pbuf.at[c], near(0, 0, 0, 1))
    for w in core_a + core_b:
        w.wait_recv()

    group_of = (iota((256, 256), 0) % 32 * 8 - 1).astype(F32)
    query_lane = iota((256, 256), 1).astype(F32)

    def score(b, _):
        sides = []
        xb, cb = b // 2, lax.rem(b, 2)
        for buf in (buf_a, buf_b):
            part = buf[xb, cb].astype(F32).reshape(32, 16, 256)
            sides += [part[:, 0:8].reshape(256, 256), part[:, 8:16].reshape(256, 256)]
        hb = jnp.concatenate([s.astype(BF16) for s in sides], axis=1)
        for n, s in enumerate(sides):
            h_t[pl.ds(n * 256, 256), pl.ds(pl.multiple_of(b * 256, 256), 256)] = s.T.astype(BF16)
        q = jnp.dot(hb, wq[...], preferred_element_type=F32)
        rq = lax.rsqrt(jnp.mean(q * q, axis=1, keepdims=True) + EPS)
        u = q * rq
        u_hi = u.astype(BF16)
        u_lo = (u - u_hi.astype(F32)).astype(BF16)
        r = rows[b]
        r32 = r.astype(F32)
        rr = lax.rsqrt(jnp.mean(r32 * r32, axis=1, keepdims=True) + EPS)
        s = (nt(r, u_hi) + nt(r, u_lo)) * (rr * SCALE)
        _row, qry = columns_of(b)
        qry = jnp.concatenate([qry, qry], axis=1)
        live = (qry > 0.5) & (group_of + qry == query_lane)
        e = jnp.where(live, jnp.exp(s), 0.0)
        zr = jnp.sum(e, axis=0, keepdims=True)
        zbuf[pl.ds(b * 2, 1), :] = zr[:, 0:128]
        zbuf[pl.ds(b * 2 + 1, 1), :] = zr[:, 128:256]
        gb = tn((e * rr).astype(BF16), r)
        gb = gb - u * (jnp.sum(u * gb, axis=1, keepdims=True) * (1.0 / E))
        ghat[pl.ds(pl.multiple_of(b * 256, 256), 256), :] = gb * (rq * SCALE)
        return 0

    lax.fori_loop(0, 8, score, 0)

    first = (lax.rem(y, 2) * 8 + z) * 8
    sub, ln = iota((8, 128), 0), iota((8, 128), 1)
    mine = jnp.sum(jnp.where(ln == first + sub, pos_exp, 0.0), axis=0, keepdims=True)
    zbuf[...] = zbuf[...] + jnp.where(iota((16, 128), 0) == blk * 2 + y // 2, mine, 0.0)

    def half(n):
        return pl.ds(pl.multiple_of(n * 8, 8), 8)

    def encode(lo, hi):
        def step(n, _):
            at = pl.ds(pl.multiple_of(n * 256, 256), 256)
            s = slab[at, :]
            p0 = pbuf[0].reshape(E, 512)
            p1_ = pbuf[1].reshape(E, 512)
            ren[at, :] = (nt(s[:, 0:512], p0) + nt(s[:, 512:1024], p1_)).astype(BF16)
            return 0

        lax.fori_loop(lo, hi, step, 0)

    w = copy(zbuf.at[half(1 - c)], zrecv.at[0], near(0, 0, 0, 1))
    loads[2].wait()
    p_c.wait_recv()
    encode(0, 1)
    w.wait_recv()
    zsum[0] = zbuf[half(c), :] + zrecv[0]
    ws = []
    for i in range(NX):
        for j in range(NY):
            if i or j:
                ws.append(copy(zsum.at[0], zrecv.at[1 + len(ws)], near(i, j, 0, 0)))
    encode(1, 4)
    total = zsum[0]
    for n, w in enumerate(ws):
        w.wait_recv()
        total = total + zrecv[1 + n]
    zsum[1] = total
    ws = [copy(zsum.at[1], zrecv.at[15 + o], near(0, 0, o, 0)) for o in range(1, NZ)]
    encode(4, 7)
    for n, w in enumerate(ws):
        w.wait_recv()
        total = total + zrecv[16 + n]
    zsum[2] = total
    w = copy(zsum.at[2], zrecv.at[23], near(0, 0, 0, 1))
    encode(7, 8)
    w.wait_recv()
    out_copy = pltpu.make_async_copy(ren, ren_hbm, local_sem.at[3])
    out_copy.start()
    other = zrecv[23]
    top = jnp.where(c == 0, total, other)
    bottom = jnp.where(c == 0, other, total)
    padded = jnp.concatenate([top, bottom, jnp.ones((112, 128), F32)], axis=0)
    turned = padded.T
    for t in range(16):
        zcol[pl.ds(t * 128, 128), :] = jnp.broadcast_to(turned[:, t:t + 1], (128, 128))

    own = pl.ds(pl.multiple_of((blk * 32 + y * 8 + z) * 8, 8), 8)
    z_own = zcol[own, :][:, 0:1]
    loss_ref[...] = jnp.broadcast_to(jnp.log(z_own) - pos_score, (8, 128))
    ghat[own, :] = ghat[own, :] + pos_dir * (pos_exp - z_own)
    own_rows = ghat[own, :] / z_own
    own_low = own_rows - own_rows.astype(BF16).astype(F32)
    own_low = jnp.concatenate([own_low, jnp.zeros_like(own_low)], axis=0).astype(BF16)
    h_pad = jnp.concatenate([h32, jnp.zeros_like(h32)], axis=0)

    def rescale(b, _):
        at = pl.ds(pl.multiple_of(b * 128, 128), 128)
        gmat[at, :] = (ghat[at, :] / zcol[at, :][:, 0:1]).astype(BF16)
        return 0

    lax.fori_loop(0, 16, rescale, 0)

    t_c = []
    for n in range(4):
        val = jnp.dot(h_t[pl.ds(n * 256, 256), :], gmat[...], preferred_element_type=F32)
        val = val + tn(h_pad[:, n * 256:(n + 1) * 256].astype(BF16), own_low)
        for t in range(6):
            tile = val[:, t * 128:(t + 1) * 128].reshape(4, 4, 16, 128)
            if X_FIRST[t]:
                tt[t, n] = tile
            else:
                for a in range(4):
                    for b in range(4):
                        tt[t, n, a, b] = tile[b, a]
        t_c.append(
            copy(tt.at[pl.ds((1 - c) * 3, 3), n], tcore.at[n], near(0, 0, 0, 1))
        )

    unit_x = [jnp.int32(1), 1 - c, jnp.int32(0)]
    first_at = [x * f + y * (1 - f) for f in unit_x]
    second_at = [y * f + x * (1 - f) for f in unit_x]
    ph1 = []
    for n in range(4):
        t_c[n].wait_recv()
        for u in range(3):
            tsum[u, n] = tt[c * 3 + u, n] + tcore[n, u]
            f = unit_x[u]
            for o in range(1, 4):
                to = lax.rem(first_at[u] + o, 4)
                ph1.append(
                    copy(tsum.at[u, n, to], r1.at[u, o - 1, n], near(o * f, o * (1 - f), 0, 0))
                )
    for u in range(3):
        for n in range(4):
            for o in range(1, 4):
                ph1[n * 9 + u * 3 + o - 1].wait_recv()
        p1[u] = tsum[u, :, first_at[u]] + r1[u, 0] + r1[u, 1] + r1[u, 2]
    ph2 = []
    for u in range(3):
        f = unit_x[u]
        for o in range(1, 4):
            to = lax.rem(second_at[u] + o, 4)
            ph2.append(copy(p1.at[u, :, to], r2.at[u, o - 1], near(o * (1 - f), o * f, 0, 0)))
    for u in range(3):
        for o in range(1, 4):
            ph2[u * 3 + o - 1].wait_recv()
        p2[:, u] = p1[u, :, second_at[u]] + r2[u, 0] + r2[u, 1] + r2[u, 2]
    ph3 = []
    for o in range(1, NZ):
        to = near(0, 0, o, 0)
        ph3.append(copy(p2.at[lax.rem(to[2], 4)], r3.at[o - 1], to))
    done = p2[zl]
    for o in range(1, NZ):
        ph3[o - 1].wait_recv()
        done = done + r3[o - 1]
    fin[y, c] = done
    ph4 = []
    for o in range(NY):
        for k in range(2):
            if o or k:
                ph4.append(copy(fin.at[y, c], fin.at[y, c], near(0, o, 0, k)))
    for w in ph4:
        w.wait_recv()
    for j in range(NY):
        for n in range(2):
            for u in range(3):
                grad_ref[pl.ds(j * 16, 16), pl.ds(n * 384 + u * 128, 128)] = fin[j, n, u]
    for w in sent:
        w.wait_send()
    out_copy.wait()


COPIES = 256


def local(
    question_encoder_states,
    query_proj,
    positive_embed,
    stale_index,
    neg_owner,
    neg_row,
    neg_count,
    slab_hidden,
    passage_projector,
):
    owner = neg_owner[..., 0]
    og, od = owner // 16, owner % 16
    oz = (og // 2) % 2 * 4 + od // 4
    code = (oz * 4 + og // 4) * 8 + od % 4 * 2 + og % 2
    live = iota(neg_row.shape, 1) < neg_count[:, None]
    code = jnp.where(live, code, -1)
    req = jnp.concatenate([code, neg_row], axis=0).astype(F32).T
    pt = jnp.transpose(passage_projector.reshape(2, 512, 48), (0, 2, 1))
    vmem = pl.BlockSpec(memory_space=pltpu.VMEM)
    hbm = pl.BlockSpec(memory_space=pl.ANY)
    V = pltpu.VMEM
    scratch = [
        V((D, E), BF16), V((2048, E), BF16), V((2048, D), BF16), V((2048, E), BF16),
        pltpu.SemaphoreType.DMA((4,)),
        V((NX, 2, NY, NZ, 16, 256), BF16), V((NX, 2, NY, NZ, 16, 256), BF16),
        V((D, 2048), BF16),
        V((NZ, NY, 8, 128), F32), V((NZ, NY, 8, 128), F32), V((NY, NZ, 8, 128), F32),
        V((8, NY * NZ, 128), F32), V((8, NY * NZ, 128), F32),
        V((2, 4, 4, 48, 512), BF16), V((8, 256, E), BF16),
        V((2048, E), F32), V((2048, E), BF16),
        V((16, 128), F32), V((24, 8, 128), F32), V((3, 8, 128), F32), V((2048, 128), F32),
        V((6, 4, 4, 4, 16, 128), F32), V((4, 3, 4, 4, 16, 128), F32),
        V((3, 4, 4, 4, 16, 128), F32),
        V((3, 3, 4, 4, 16, 128), F32), V((3, 4, 4, 16, 128), F32),
        V((3, 3, 4, 16, 128), F32), V((4, 3, 16, 128), F32),
        V((NZ - 1, 3, 16, 128), F32), V((NY, 2, 3, 16, 128), F32),
        pltpu.SemaphoreType.DMA((COPIES,)), pltpu.SemaphoreType.DMA((COPIES,)),
    ]
    losses, grad, renewed = pl.pallas_call(
        body,
        out_shape=(
            jax.ShapeDtypeStruct((8, 128), F32),
            jax.ShapeDtypeStruct((64, E), F32),
            jax.ShapeDtypeStruct((2048, E), BF16),
        ),
        in_specs=[vmem, vmem, vmem, vmem, hbm, hbm, hbm],
        out_specs=(vmem, vmem, hbm),
        scratch_shapes=scratch,
        compiler_params=pltpu.CompilerParams(
            collective_id=0, has_side_effects=True, vmem_limit_bytes=62 * 2**20
        ),
        cost_estimate=pl.CostEstimate(
            flops=30 * 10**9, bytes_accessed=16 * 2**20, transcendentals=2**20
        ),
    )(question_encoder_states, req, positive_embed, pt, query_proj, stale_index, slab_hidden)
    return losses[:, 0], grad, renewed


def solution(mesh):
    rows = P(("group", "dev"), None)
    in_specs = (
        rows, P(), rows, rows, P(("group", "dev"), None, None), rows,
        P(("group", "dev")), rows, P(None, "dev"),
    )
    out_specs = (P(("group", "dev")), P("dev", None), rows)
    return jax.shard_map(local, mesh=mesh, in_specs=in_specs, out_specs=out_specs, check_vma=False)
```

time: 524 us -> 125 us (0.24)
  waiting for transfers between devices: 336 us -> 0 us
  Pallas kernels: 0 us -> 114 us
  blocking collectives: 106 us -> 0 us
  local copies, waits for them, and re-layouts: 29.5 us -> 8.94 us
  matrix products: 18.8 us -> 0 us
  between operations: 15.7 us -> 0.64 us
  starting transfers between devices: 7.63 us -> 0 us
  other arithmetic: 8.64 us -> 1.45 us
    psum x1 -> x0, waiting for transfers between devices: 263 us -> none  [local(): summed = lax.psum(grad_term, ('group', 'dev'))]
    pallas_call x0 -> x1, Pallas kernels: none -> 114 us  [local(): pl.pallas_call(body, out_shape=(jax.ShapeDtypeStruct((8, 128), F32), jax....]
    all_to_all x3 -> x0, blocking collectives: 106 us -> none  [the longest x1 72.2 us: local(): lax.all_to_all(picked, 'dev', split_axis=1, concat_axis=1, tiled=True)]
    all_to_all x1 -> x0, waiting for transfers between devices: 59.2 us -> none  [local(): lax.all_to_all(answered, 'group', split_axis=0, concat_axis=0, tiled=True)]
    dot_general x5 -> x0, matrix products: 18.8 us -> none  [the longest x1 7.84 us: local(): jnp.dot(slab_hidden, lax.all_gather(passage_projector, 'dev', axis=1, til...]
    gather x2 -> x0, local copies, waits for them, and re-layouts: 17.3 us -> none  [the longest x1 9.4 us: local(): jnp.take(stale_index, asked.reshape(-1), axis=0)]
    all_gather x1 -> x0, waiting for transfers between devices: 13.4 us -> none  [local(): lax.all_gather(passage_projector, 'dev', axis=1, tiled=True)]
    all_to_all x1 -> x0, starting transfers between devices: 7.37 us -> none  [local(): lax.all_to_all(answered, 'group', split_axis=0, concat_axis=0, tiled=True)]
  transfers between devices with their start and end apart: 3 -> 0, of which waited for: 3 -> 0; matrix products, arithmetic and copies ran while one was open for 6% -> 0% of each run, Pallas kernels for 0% -> 0%
where the time goes in v1:
time: 125 us
  Pallas kernels  114 us (91%)
  local copies, waits for them, and re-layouts  8.94 us (7%)
  other arithmetic  1.45 us (1%)
    pallas_call x1, Pallas kernels, local(): pl.pallas_call(body, out_shape=(jax.ShapeDtypeStruct((8, 128), F32), jax....  114 us
    unnamed x2, local copies, waits for them, and re-layouts  5.37 us

profile of v1, /device:TPU:1, one launch (start us, length us, event | category | flops | bytes accessed | tf_op | source)
XLA Modules:
  0.0 125.0 jit_solution(4710132446985079134)
XLA Ops:
  0.6 0.8 fusion.8
  1.4 0.7 add_convert_fusion
  2.1 0.7 copy.17
  2.8 1.5 %copy.21 = bf16[6,2,8,512]{3,2,0,1:T(8,128)(2,1)} copy(bf16[6,2,8,512]{3,2,1,0:T(8,128)(2,1)} %bitcast.9) | data formatting | bytes 196608 | tf_op jit(solution)/shard_map/reshape | solution.py:425
  4.4 114.0 %shard_map.112 = (f32[8,128]{1,0:T(8,128)}, f32[64,768]{1,0:T(8,128)}, bf16[2048,768]{1,0:T(8,128)(2,1)}) custom-call(bf16[8,1024]{1,0:T(8,128)(2,1)} %h_ref.1, f32[128,16]{1,0:T(8,128)} %bitcast.11, bf16[8,768]{1,0:T(8,128)(2,1)} %pos_ref.1, bf16[2,48,512]{2,1,0:T(8,128)(2,1)} %bitcast.10, bf16[1024,768]{1,0:T(8,128)(2,1)} %wq_hbm.1, ...), custom_call_target="tpu_custom_call" | custom-call | flops 30000001024 | bytes 16777216 | tf_op jit(solution)/shard_map/pallas_call | solution.py:446
  118.3 1.3 %slice_reduce_fusion = f32[8]{0:T(128)} fusion(f32[8,128]{1,0:T(8,128)} %get-tuple-element.6), kind=kLoop, calls=%fused_computation.34 | loop fusion | bytes 64 | tf_op jit(solution)/shard_map/slice | solution.py:463
  119.6 1.6 %copy.24 = f32[64,768]{1,0:T(8,128)} copy(f32[64,768]{1,0:T(8,128)} %get-tuple-element.13) | data formatting | bytes 393216
  121.2 3.8 %copy.25 = bf16[2048,768]{1,0:T(8,128)(2,1)} copy(bf16[2048,768]{1,0:T(8,128)(2,1)} %get-tuple-element.14) | data formatting | bytes 6291456

commit v2 on v0

v2 whole, which is shorter than its diff:
```python
import jax
import jax.numpy as jnp
from jax import lax
from jax.experimental import pallas as pl
from jax.experimental.pallas import tpu as pltpu
from jax.sharding import PartitionSpec as P

MESH = pl.DeviceIdType.MESH
F32 = jnp.float32
BF16 = jnp.bfloat16
EPS = 1e-06
DIV = 0.05
E = 768
D = 1024
SCALE = 1.0 / (E * DIV)
NX, NY, NZ = 4, 4, 8
X_FIRST = (True, True, False, True, False, False)


def iota(shape, dim):
    return lax.broadcasted_iota(jnp.int32, shape, dim)


def nt(a, b):
    return lax.dot_general(a, b, (((1,), (1,)), ((), ())), preferred_element_type=F32)


def tn(a, b):
    return lax.dot_general(a, b, (((0,), (0,)), ((), ())), preferred_element_type=F32)


def device_of(x, y, z, c):
    return ((y * 2 + z // 4) * 2 + c, lax.rem(z, 4) * 4 + x)


def body(
    h_ref, owner_ref, row_ref, count_ref, pos_ref, pt_ref, wq_hbm, idx_hbm, slab_hbm,
    loss_ref, grad_ref, ren_hbm,
    wq, idx, slab, ren, local_sem,
    buf_a, buf_b, h_t, tab, tab_y, tab_j, tab_r,
    pbuf, rows, norm, u_two, u_scale, ghat, gmat, zbuf, zrecv, zsum, zcol,
    tt, tcore, tsum, r1, p1, r2, p2, r3, fin,
    ssem, rsem,
):
    g = lax.axis_index("group")
    d = lax.axis_index("dev")
    x = lax.rem(d, 4)
    c = lax.rem(g, 2)
    y = g // 4
    zl = d // 4
    z = lax.rem(g // 2, 2) * 4 + zl

    def near(dx, dy, dz, dc):
        return (
            lax.rem(x + dx + NX, NX),
            lax.rem(y + dy + NY, NY),
            lax.rem(z + dz + NZ, NZ),
            lax.rem(c + dc, 2),
        )

    used_s, used_r, sends = [0], [0], []

    def send_sem(ref):
        n = used_s[0]
        used_s[0] = n + 1
        sends.append((ssem.at[n], ref))
        return ssem.at[n]

    def recv_sem():
        n = used_r[0]
        used_r[0] = n + 1
        return rsem.at[n]

    def await_bytes(sem, ref):
        pltpu.make_async_copy(ref, ref, sem).wait()

    def copy(src, dst, at, s_sem, r_sem):
        pltpu.make_async_remote_copy(
            src_ref=src, dst_ref=dst, send_sem=s_sem, recv_sem=r_sem,
            device_id=device_of(*at), device_id_type=MESH,
        ).start()

    peers = [(0, 0, i, 0) for i in range(1, NZ)]
    peers += [(i, j, 0, 0) for i in range(NX) for j in range(NY) if i or j]
    peers += [(0, 0, i, 1) for i in range(NZ)]
    peers += [(0, j, 0, 1) for j in range(1, NY)]
    barrier = pltpu.get_barrier_semaphore()
    for p in peers:
        pl.semaphore_signal(barrier, inc=1, device_id=device_of(*near(*p)), device_id_type=MESH)

    h32 = h_ref[...].astype(F32)
    buf_a[x, c, y, z] = jnp.concatenate([h32[:, 0:256], h32[:, 256:512]], axis=0).astype(BF16)
    buf_b[x, c, y, z] = jnp.concatenate([h32[:, 512:768], h32[:, 768:1024]], axis=0).astype(BF16)
    pbuf[c, zl, x] = jnp.where(
        c == 0, pt_ref[:, 0:512].astype(F32), pt_ref[:, 512:1024].astype(F32)
    ).astype(BF16)
    loads = []
    for n, (src, dst) in enumerate(((wq_hbm, wq), (idx_hbm, idx), (slab_hbm, slab))):
        load = pltpu.make_async_copy(src, dst, local_sem.at[n])
        loads.append(load)
    loads[0].start()
    loads[1].start()

    owner = owner_ref[...]
    og, od = owner >> 4, owner & 15
    code = ((od & 3) * 4 + (og >> 2)) * 16 + (((og >> 1) & 1) * 4 + (od >> 2)) * 2 + (og & 1)
    sub, ln = iota((8, 128), 0), iota((8, 128), 1)
    count = jnp.zeros((8, 128), jnp.int32)
    for i in range(8):
        count = jnp.where(sub == i, count_ref[i], count)
    code = jnp.where(ln < count, code, -1).astype(F32)
    row = row_ref[...].astype(F32)
    high = jnp.floor(row * (1.0 / 16.0))
    low = row - 16.0 * high
    line = iota((128, 128), 0)
    kind, place = line % 16, line // 16
    upper = (line < iota((128, 128), 1)).astype(F32).astype(BF16)
    owner_line = iota((256, 128), 0).astype(F32)
    hits = [(code[i:i + 1] == owner_line).astype(F32) for i in range(8)]
    before = [jnp.dot(t.astype(BF16), upper, preferred_element_type=F32) for t in hits]
    totals = [jnp.sum(t, axis=1, keepdims=True) for t in hits]
    carry = jnp.zeros((256, 1), F32)
    table = jnp.zeros((256, 128), F32)
    for i in range(8):
        rank = jnp.sum(hits[i] * (before[i] + carry), axis=0, keepdims=True)
        carry = carry + totals[i]
        value = jnp.where(kind == 0, high[i:i + 1], jnp.where(kind == 1, low[i:i + 1], jnp.where(kind == 2, i + 1.0, 0.0)))
        value = jnp.where(rank == place.astype(F32), value, 0.0)
        table = table + nt(hits[i].astype(BF16), value.astype(BF16))
    tab[...] = table.astype(BF16).reshape(16, 16, 128)
    pl.semaphore_wait(barrier, len(peers))

    bufs = (buf_a, buf_b)
    z_sem = []
    for buf in bufs:
        s, r = send_sem(buf.at[0, 0, 0, 0:7]), recv_sem()
        for o in range(1, NZ):
            copy(buf.at[x, c, y, z], buf.at[x, c, y, z], near(0, 0, o, 0), s, r)
        z_sem.append(r)
    s, px_sem = send_sem(pbuf.at[0, 0, 0:3]), recv_sem()
    for o in range(1, NX):
        copy(pbuf.at[c, zl, x], pbuf.at[c, zl, x], near(o, 0, 0, 0), s, px_sem)

    spot = x * 4 + y
    s, ty_sem = send_sem(tab_y.at[0:15]), recv_sem()
    for i in range(NX):
        for j in range(NY):
            if i or j:
                to = near(i, j, 0, 0)
                copy(tab.at[to[0] * 4 + to[1]], tab_y.at[spot], to, s, ty_sem)
    tab_y[spot] = tab[spot]

    loads[2].start()

    loads[0].wait()
    q_own = jnp.dot(h_ref[...], wq[...], preferred_element_type=F32)
    rq_own = lax.rsqrt(jnp.mean(q_own * q_own, axis=1, keepdims=True) + EPS)
    u_own = q_own * rq_own
    pos = pos_ref[...].astype(F32)
    pos = pos * lax.rsqrt(jnp.mean(pos * pos, axis=1, keepdims=True) + EPS)
    pos_dot = jnp.sum(u_own * pos, axis=1, keepdims=True)
    pos_score = pos_dot * SCALE
    pos_exp = jnp.exp(pos_score)
    pos_dir = (pos - u_own * (pos_dot * (1.0 / E))) * (rq_own * SCALE)

    def along_x(o):
        return (o, 0, 0, 0)

    def along_y(o):
        return (0, o, 0, 0)

    mid_axis, last_axis = (along_y, along_x), (along_x, along_y)
    mid_sem, near_sem, far_sem, core_sem = [], [], [], []
    s_mid, s_near, s_far, s_core = [], [], [], []
    for buf in bufs:
        mid_sem.append([recv_sem() for _ in range(3)])
        near_sem.append([recv_sem() for _ in range(4)])
        far_sem.append(recv_sem())
        core_sem.append(recv_sem())
        s_mid.append(send_sem(buf.at[0, 0, 0:3]))
        s_near.append(send_sem(buf.at[:, 0, 0:2]))
        s_far.append(send_sem(buf.at[:, 0, 0]))
        s_core.append(send_sem(buf.at[:, 0]))

    def group(n, j, q):
        if n == 0:
            return buf_a.at[lax.rem(x - q + NX, NX), c, lax.rem(y - j + NY, NY)]
        return buf_b.at[lax.rem(x - j + NX, NX), c, lax.rem(y - q + NY, NY)]

    def to_core(n, ref):
        copy(ref, ref, near(0, 0, 0, 1), s_core[n], core_sem[n])

    def to_near(n, j):
        ref = group(n, j, 0)
        for o in (1, 3):
            copy(ref, ref, near(*last_axis[n](o)), s_near[n], near_sem[n][j])
        to_core(n, ref)

    def forward(n, j):
        await_bytes(near_sem[n][j], bufs[n].at[0, 0, 0:2])
        ahead, behind = group(n, j, 1), group(n, j, 3)
        lo, hi = ahead.at[0:4], behind.at[4:8]
        copy(lo, lo, near(*last_axis[n](1)), s_far[n], far_sem[n])
        copy(hi, hi, near(*last_axis[n](3)), s_far[n], far_sem[n])
        to_core(n, ahead)
        to_core(n, behind)

    for n, buf in enumerate(bufs):
        await_bytes(z_sem[n], buf.at[0, 0, 0, 0:7])
        ref = group(n, 0, 0)
        for o in range(1, 4):
            copy(ref, ref, near(*mid_axis[n](o)), s_mid[n], mid_sem[n][o - 1])
        to_near(n, 0)

    await_bytes(ty_sem, tab_y.at[0:15])
    tab_j[...] = jnp.swapaxes(tab_y[...].astype(F32), 0, 1).astype(BF16)
    s, tj_sem = send_sem(tab_r.at[0:15]), recv_sem()
    for o in range(NZ):
        for k in range(2):
            if o or k:
                to = near(0, 0, o, k)
                copy(tab_j.at[to[2] * 2 + to[3]], tab_r.at[z * 2 + c], to, s, tj_sem)
    tab_r[z * 2 + c] = tab_j[z * 2 + c]

    await_bytes(px_sem, pbuf.at[0, 0, 0:3])
    s, pz_sem = send_sem(pbuf.at[0, 0:3]), recv_sem()
    for o in (1, 7):
        copy(pbuf.at[c, zl], pbuf.at[c, zl], near(0, 0, o, 0), s, pz_sem)
    copy(pbuf.at[c, zl, 0:2], pbuf.at[c, zl, 0:2], near(0, 0, 2, 0), s, pz_sem)
    copy(pbuf.at[c, zl, 2:4], pbuf.at[c, zl, 2:4], near(0, 0, 6, 0), s, pz_sem)

    def middle(o):
        for n in range(2):
            await_bytes(mid_sem[n][o - 1], bufs[n].at[0, 0, 0])
            to_near(n, o)

    middle(1)
    middle(3)

    loads[1].wait()
    await_bytes(tj_sem, tab_r.at[0:15])
    src, out = iota((128, 2048), 0), iota((128, 2048), 1)
    slot, want_q = out // 256, (out // 128) % 2
    weight = jnp.where(src % 16 == 0, 16.0, 1.0)
    kept = jnp.where(want_q == 0, jnp.where(src % 16 < 2, weight, 0.0), jnp.where(src % 16 == 2, 1.0, 0.0))
    expand = jnp.where(src // 16 == slot, kept, 0.0).astype(BF16)

    def columns_of(b):
        wide = jnp.dot(tab_r[2 * b:2 * b + 2].reshape(32, 128), expand, preferred_element_type=F32)
        row = jnp.concatenate([wide[:, k * 256:k * 256 + 128] for k in range(8)], axis=0)
        qry = jnp.concatenate([wide[:, k * 256 + 128:k * 256 + 256] for k in range(8)], axis=0)
        return row, qry

    lane_f = iota((256, 128), 1).astype(F32)

    def pick(b):
        row, qry = columns_of(b)
        hot = jnp.concatenate(
            [(row == lane_f + 128.0 * t).astype(F32).astype(BF16) for t in range(16)], axis=1
        )
        r = jnp.dot(hot, idx[...], preferred_element_type=F32)
        rows[b] = r.astype(BF16)
        rr = lax.rsqrt(jnp.mean(r * r, axis=1, keepdims=True) + EPS)
        norm[b, 0] = jnp.broadcast_to(rr, (256, 128))
        norm[b, 1] = qry

    def onward(j):
        for n in range(2):
            forward(n, j)

    pick(0)
    middle(2)
    pick(1)
    onward(0)
    pick(2)
    onward(1)
    pick(3)
    pick(4)
    onward(3)
    await_bytes(pz_sem, pbuf.at[0, 0:3])
    s, pc_sem = send_sem(pbuf.at[0]), recv_sem()
    copy(pbuf.at[c], pbuf.at[c], near(0, 0, 0, 1), s, pc_sem)
    pick(5)
    onward(2)
    pick(6)
    pick(7)
    for n, buf in enumerate(bufs):
        await_bytes(far_sem[n], buf.at[:, 0, 0])
        for j in range(4):
            to_core(n, group(n, j, 2))
    for n, buf in enumerate(bufs):
        await_bytes(core_sem[n], buf.at[:, 0])

    def project(b, _):
        sides = []
        for buf in bufs:
            part = jnp.swapaxes(buf[:, :, :, b], 0, 1).astype(F32).reshape(32, 16, 256)
            sides += [part[:, 0:8].reshape(256, 256), part[:, 8:16].reshape(256, 256)]
        sides = [t.astype(BF16) for t in sides]
        for n, t in enumerate(sides):
            h_t[pl.ds(n * 256, 256), pl.ds(pl.multiple_of(b * 256, 256), 256)] = t.T
        q = jnp.dot(jnp.concatenate(sides, axis=1), wq[...], preferred_element_type=F32)
        rq = lax.rsqrt(jnp.mean(q * q, axis=1, keepdims=True) + EPS)
        u = q * rq
        hi = u.astype(BF16)
        u_two[b, 0:256] = hi
        u_two[b, 256:512] = (u - hi.astype(F32)).astype(BF16)
        u_scale[b] = jnp.broadcast_to(rq * SCALE, (256, 128))
        return 0

    lax.fori_loop(0, 8, project, 0, unroll=4)

    group_of = (iota((256, 256), 0) % 32 * 8 - 1).astype(F32)
    query_lane = iota((256, 256), 1).astype(F32)

    def score(b, _):
        r = rows[b]
        two = u_two[b]
        rr = norm[b, 0][:, 0:1]
        s = nt(two, r)
        s = (s[0:256] + s[256:512]).T * (rr * SCALE)
        qry = jnp.concatenate([norm[b, 1], norm[b, 1]], axis=1)
        live = (qry > 0.5) & (group_of + qry == query_lane)
        e = jnp.where(live, jnp.exp(s), 0.0)
        zr = jnp.sum(e, axis=0, keepdims=True)
        zbuf[b // 4, pl.ds(lax.rem(b, 4) * 2, 1), :] = zr[:, 0:128]
        zbuf[b // 4, pl.ds(lax.rem(b, 4) * 2 + 1, 1), :] = zr[:, 128:256]
        gb = tn((e * rr).astype(BF16), r)
        u = two[0:256].astype(F32) + two[256:512].astype(F32)
        gb = gb - u * (jnp.sum(u * gb, axis=1, keepdims=True) * (1.0 / E))
        ghat[pl.ds(pl.multiple_of(b * 256, 256), 256), :] = gb * u_scale[b][:, 0:1]
        return 0

    own_at = ((z * 2 + c) * 16 + x * 4 + y) * 8
    mine = jnp.sum(jnp.where(ln == lax.rem(own_at, 128) + sub, pos_exp, 0.0), axis=0, keepdims=True)
    z_sems = []

    def sums_core(k):
        zbuf[k] = zbuf[k] + jnp.where(sub + 8 * k == own_at // 128, mine, 0.0)
        s, r = send_sem(zrecv.at[k, 0]), recv_sem()
        copy(zbuf.at[k], zrecv.at[k, 0], near(0, 0, 0, 1), s, r)
        z_sems.append(r)

    def sums_xy(k):
        await_bytes(z_sems[k], zrecv.at[k, 0])
        zsum[k, 0] = zbuf[k] + zrecv[k, 0]
        s, r = send_sem(zrecv.at[k, 1:16]), recv_sem()
        n = 1
        for i in range(NX):
            for j in range(NY):
                if i or j:
                    copy(zsum.at[k, 0], zrecv.at[k, n], near(i, j, 0, 0), s, r)
                    n += 1
        return r

    def sums_z(k, r):
        await_bytes(r, zrecv.at[k, 1:16])
        total = zsum[k, 0]
        for n in range(1, 16):
            total = total + zrecv[k, n]
        zsum[k, 1] = total
        s, r = send_sem(zrecv.at[k, 16:23]), recv_sem()
        for o in range(1, NZ):
            copy(zsum.at[k, 1], zrecv.at[k, 15 + o], near(0, 0, o, 0), s, r)
        return r

    def sums_done(k, r):
        await_bytes(r, zrecv.at[k, 16:23])
        total = zsum[k, 1]
        for n in range(16, 23):
            total = total + zrecv[k, n]
        turned = jnp.concatenate([total, jnp.ones((120, 128), F32)], axis=0).T
        for t in range(8):
            zcol[pl.ds(k * 1024 + t * 128, 128), :] = jnp.broadcast_to(
                turned[:, t:t + 1], (128, 128)
            )

    def encode(lo, hi):
        def step(n, _):
            at = pl.ds(pl.multiple_of(n * 256, 256), 256)
            t = slab[at, :]
            q0, q1 = pbuf[0].reshape(E, 512), pbuf[1].reshape(E, 512)
            ren[at, :] = (nt(t[:, 0:512], q0) + nt(t[:, 512:1024], q1)).astype(BF16)
            return 0

        lax.fori_loop(lo, hi, step, 0)

    own = pl.ds(pl.multiple_of(own_at, 8), 8)

    def rescale(k):
        @pl.when(own_at // 1024 == k)
        def _():
            z_here = zcol[own, :][:, 0:1]
            ghat[own, :] = ghat[own, :] + pos_dir * (pos_exp - z_here)

        def step(b, _):
            at = pl.ds(pl.multiple_of(b * 128, 128), 128)
            gmat[at, :] = (ghat[at, :] / zcol[at, :][:, 0:1]).astype(BF16)
            return 0

        lax.fori_loop(k * 8, k * 8 + 8, step, 0)

    unit_x = [jnp.int32(1), 1 - c, jnp.int32(0)]
    first_at = [x * f + y * (1 - f) for f in unit_x]
    second_at = [y * f + x * (1 - f) for f in unit_x]
    quarter = [lax.rem(zl + 1 + n, 4) for n in range(4)]

    def product(n, k):
        at = pl.ds(pl.multiple_of(quarter[n] * 256, 256), 256)
        span = pl.ds(k * 1024, 1024)
        return jnp.dot(h_t[at, span], gmat[span, :], preferred_element_type=F32)

    def keep(n, val, more):
        for t in range(6):
            tile = val[:, t * 128:(t + 1) * 128].reshape(4, 4, 16, 128)
            if X_FIRST[t]:
                tt[n, t] = tt[n, t] + tile if more else tile
            else:
                for a in range(4):
                    for b in range(4):
                        part = tile[b, a]
                        tt[n, t, a, b] = tt[n, t, a, b] + part if more else part

    lax.fori_loop(0, 4, score, 0, unroll=4)
    sums_core(0)
    lax.fori_loop(4, 6, score, 0, unroll=2)
    xy_0 = sums_xy(0)
    lax.fori_loop(6, 8, score, 0, unroll=2)
    sums_core(1)
    za_0 = sums_z(0, xy_0)
    loads[2].wait()
    await_bytes(pc_sem, pbuf.at[0])
    encode(0, 2)
    xy_1 = sums_xy(1)
    encode(2, 5)
    sums_done(0, za_0)
    rescale(0)
    keep(0, product(0, 0), False)
    za_1 = sums_z(1, xy_1)
    for n in range(1, 4):
        keep(n, product(n, 0), False)
    encode(5, 8)
    out_copy = pltpu.make_async_copy(ren, ren_hbm, local_sem.at[3])
    out_copy.start()
    sums_done(1, za_1)
    rescale(1)

    z_own = zcol[own, :][:, 0:1]
    loss = jnp.log(z_own) - pos_score
    loss_ref[...] = jnp.sum(jnp.where(sub == ln, loss, 0.0), axis=0, keepdims=True)[:, 0:8]
    own_rows = ghat[own, :] / z_own
    own_low = own_rows - own_rows.astype(BF16).astype(F32)
    own_low = jnp.concatenate([own_low, jnp.zeros_like(own_low)], axis=0).astype(BF16)
    h_pad = jnp.concatenate([h32, jnp.zeros_like(h32)], axis=0)
    h_pad = jnp.concatenate(
        [h_pad[:, n * 256:(n + 1) * 256] for n in range(4)], axis=0
    ).astype(BF16)

    s_tc, tc_sem = send_sem(tcore), [recv_sem() for _ in range(4)]
    s_r1, r1_sem = send_sem(r1), [recv_sem() for _ in range(4)]
    s_r2, r2_sem = send_sem(r2), [recv_sem() for _ in range(4)]
    s_r3, r3_sem = send_sem(r3), recv_sem()
    hpt = h_pad.reshape(4, 16, 256)

    def produce(n):
        val = product(n, 1)
        mine = jnp.zeros((16, 256), F32)
        for t in range(4):
            mine = jnp.where(quarter[n] == t, hpt[t].astype(F32), mine)
        val = val + tn(mine.astype(BF16), own_low)
        keep(n, val, True)
        copy(tt.at[n, pl.ds((1 - c) * 3, 3)], tcore.at[n], near(0, 0, 0, 1), s_tc, tc_sem[n])

    def step_first(n):
        await_bytes(tc_sem[n], tcore.at[n])
        for u in range(3):
            f = unit_x[u]
            tsum[n, u] = tt[n, c * 3 + u] + tcore[n, u]
            for o in range(1, 4):
                to = lax.rem(first_at[u] + o, 4)
                copy(
                    tsum.at[n, u, to], r1.at[n, u, o - 1], near(o * f, o * (1 - f), 0, 0),
                    s_r1, r1_sem[n],
                )

    def step_second(n):
        await_bytes(r1_sem[n], r1.at[n])
        for u in range(3):
            f = unit_x[u]
            p1[n, u] = tsum[n, u, first_at[u]] + (r1[n, u, 0] + r1[n, u, 1] + r1[n, u, 2])
            for o in range(1, 4):
                to = lax.rem(second_at[u] + o, 4)
                copy(
                    p1.at[n, u, to], r2.at[n, u, o - 1], near(o * (1 - f), o * f, 0, 0),
                    s_r2, r2_sem[n],
                )

    def step_z(n):
        await_bytes(r2_sem[n], r2.at[n])
        for u in range(3):
            p2[n, u] = p1[n, u, second_at[u]] + (r2[n, u, 0] + r2[n, u, 1] + r2[n, u, 2])
        for k in range(2):
            if n < 3 or k:
                to = lax.rem(zl + n + 1, 4) + 4 * k
                if n == 3:
                    to = lax.rem(z + 4, 8)
                away = lax.rem(to - z + NZ, NZ)
                copy(p2.at[n], r3.at[away - 1], (x, y, to, c), s_r3, r3_sem)

    produce(0)
    produce(1)
    step_first(0)
    produce(2)
    step_first(1)
    produce(3)
    step_first(2)
    step_second(0)
    step_first(3)
    step_second(1)
    step_z(0)
    step_second(2)
    step_z(1)
    step_second(3)
    step_z(2)
    step_z(3)
    await_bytes(r3_sem, r3)
    done = p2[3]
    for o in range(NZ - 1):
        done = done + r3[o]
    at = y * 2 + c
    fin[at] = done
    s, r = send_sem(fin.at[0:7]), recv_sem()
    for o in range(NY):
        for k in range(2):
            if o or k:
                copy(fin.at[at], fin.at[at], near(0, o, 0, k), s, r)
    await_bytes(r, fin.at[0:7])
    for j in range(NY):
        for n in range(2):
            for u in range(3):
                grad_ref[pl.ds(j * 16, 16), pl.ds(n * 384 + u * 128, 128)] = fin[j * 2 + n, u]
    for sem, ref in sends:
        await_bytes(sem, ref)
    out_copy.wait()
    assert (used_s[0], used_r[0]) == (SENDS, RECVS)


def hand_over(loss_in, grad_in, ren_in, loss_out, grad_out, ren_out, held, sem):
    parts = 4
    size = ren_in.shape[0] // parts
    ins, outs = [], []
    for n in range(parts):
        at = pl.ds(n * size, size)
        ins.append(pltpu.make_async_copy(ren_in.at[at], held.at[at], sem.at[n]))
        outs.append(pltpu.make_async_copy(held.at[at], ren_out.at[at], sem.at[parts + n]))
    for copy in ins:
        copy.start()
    loss_out[...] = loss_in[...]
    grad_out[...] = grad_in[...]
    for first, then in zip(ins, outs):
        first.wait()
        then.start()
    for copy in outs:
        copy.wait()


SENDS = 26
RECVS = 45


def local(
    question_encoder_states,
    query_proj,
    positive_embed,
    stale_index,
    neg_owner,
    neg_row,
    neg_count,
    slab_hidden,
    passage_projector,
):
    vmem = pl.BlockSpec(memory_space=pltpu.VMEM)
    smem = pl.BlockSpec(memory_space=pltpu.SMEM)
    hbm = pl.BlockSpec(memory_space=pl.ANY)
    V = pltpu.VMEM
    scratch = [
        V((D, E), BF16), V((2048, E), BF16), V((2048, D), BF16), V((2048, E), BF16),
        pltpu.SemaphoreType.DMA((4,)),
        V((NX, 2, NY, NZ, 16, 256), BF16), V((NX, 2, NY, NZ, 16, 256), BF16),
        V((D, 2048), BF16),
        V((16, 16, 128), BF16), V((16, 16, 128), BF16), V((16, 16, 128), BF16),
        V((16, 16, 128), BF16),
        V((2, 4, 4, 48, 512), BF16), V((8, 256, E), BF16), V((8, 2, 256, 128), F32),
        V((8, 512, E), BF16), V((8, 256, 128), F32),
        V((2048, E), F32), V((2048, E), BF16),
        V((2, 8, 128), F32), V((2, 23, 8, 128), F32), V((2, 2, 8, 128), F32), V((2048, 128), F32),
        V((4, 6, 4, 4, 16, 128), F32), V((4, 3, 4, 4, 16, 128), F32),
        V((4, 3, 4, 4, 16, 128), F32),
        V((4, 3, 3, 4, 16, 128), F32), V((4, 3, 4, 16, 128), F32),
        V((4, 3, 3, 16, 128), F32), V((4, 3, 16, 128), F32),
        V((NZ - 1, 3, 16, 128), F32), V((NY * 2, 3, 16, 128), F32),
        pltpu.SemaphoreType.DMA((SENDS,)), pltpu.SemaphoreType.DMA((RECVS,)),
    ]
    shapes = (
        jax.ShapeDtypeStruct((1, 8), F32),
        jax.ShapeDtypeStruct((64, E), F32),
        jax.ShapeDtypeStruct((2048, E), BF16),
    )
    results = pl.pallas_call(
        body,
        out_shape=shapes,
        in_specs=[vmem, vmem, vmem, smem, vmem, vmem, hbm, hbm, hbm],
        out_specs=(vmem, vmem, hbm),
        scratch_shapes=scratch,
        compiler_params=pltpu.CompilerParams(
            collective_id=0, has_side_effects=True, vmem_limit_bytes=62 * 2**20
        ),
        cost_estimate=pl.CostEstimate(
            flops=30 * 10**9, bytes_accessed=16 * 2**20, transcendentals=2**20
        ),
    )(
        question_encoder_states, neg_owner[..., 0], neg_row, neg_count, positive_embed,
        passage_projector.T, query_proj, stale_index, slab_hidden,
    )
    losses, grad, renewed = pl.pallas_call(
        hand_over,
        out_shape=shapes,
        in_specs=[vmem, vmem, hbm],
        out_specs=(vmem, vmem, hbm),
        scratch_shapes=[V((2048, E), BF16), pltpu.SemaphoreType.DMA((8,))],
        compiler_params=pltpu.CompilerParams(vmem_limit_bytes=62 * 2**20),
    )(*results)
    return losses.reshape(8), grad, renewed


def solution(mesh):
    rows = P(("group", "dev"), None)
    in_specs = (
        rows, P(), rows, rows, P(("group", "dev"), None, None), rows,
        P(("group", "dev")), rows, P(None, "dev"),
    )
    out_specs = (P(("group", "dev")), P("dev", None), rows)
    return jax.shard_map(local, mesh=mesh, in_specs=in_specs, out_specs=out_specs, check_vma=False)
```

time: 524 us -> 99.1 us (0.19)
  waiting for transfers between devices: 336 us -> 0 us
  blocking collectives: 106 us -> 0 us
  Pallas kernels: 0 us -> 98.1 us
  local copies, waits for them, and re-layouts: 29.5 us -> 0 us
  matrix products: 18.8 us -> 0 us
  between operations: 15.7 us -> 0.82 us
  other arithmetic: 8.64 us -> 0 us
  starting transfers between devices: 7.63 us -> 0 us
    psum x1 -> x0, waiting for transfers between devices: 263 us -> none  [local(): summed = lax.psum(grad_term, ('group', 'dev'))]
    all_to_all x3 -> x0, blocking collectives: 106 us -> none  [the longest x1 72.2 us: local(): lax.all_to_all(picked, 'dev', split_axis=1, concat_axis=1, tiled=True)]
    pallas_call x0 -> x2, Pallas kernels: none -> 98.1 us  [the longest x1 93.6 us: local(): pl.pallas_call(body, out_shape=shapes, in_specs=[vmem, vmem, vmem, smem,...]
    all_to_all x1 -> x0, waiting for transfers between devices: 59.2 us -> none  [local(): lax.all_to_all(answered, 'group', split_axis=0, concat_axis=0, tiled=True)]
    dot_general x5 -> x0, matrix products: 18.8 us -> none  [the longest x1 7.84 us: local(): jnp.dot(slab_hidden, lax.all_gather(passage_projector, 'dev', axis=1, til...]
    gather x2 -> x0, local copies, waits for them, and re-layouts: 17.3 us -> none  [the longest x1 9.4 us: local(): jnp.take(stale_index, asked.reshape(-1), axis=0)]
    all_gather x1 -> x0, waiting for transfers between devices: 13.4 us -> none  [local(): lax.all_gather(passage_projector, 'dev', axis=1, tiled=True)]
    all_to_all x1 -> x0, starting transfers between devices: 7.37 us -> none  [local(): lax.all_to_all(answered, 'group', split_axis=0, concat_axis=0, tiled=True)]
  transfers between devices with their start and end apart: 3 -> 0, of which waited for: 3 -> 0; matrix products, arithmetic and copies ran while one was open for 6% -> 0% of each run, Pallas kernels for 0% -> 0%
where the time goes in v2:
time: 99.1 us; the launch traced here: 98.9 us
  Pallas kernels  98.1 us (99%)
    pallas_call x1, Pallas kernels, local(): pl.pallas_call(body, out_shape=shapes, in_specs=[vmem, vmem, vmem, smem,...  93.6 us
    pallas_call x1, Pallas kernels, local(): pl.pallas_call(hand_over, out_shape=shapes, in_specs=[vmem, vmem, hbm], o...  4.47 us

profile of v2, /device:TPU:1, one launch (start us, length us, event | category | flops | bytes accessed | tf_op | source)
XLA Modules:
  0.0 98.9 jit_solution(5812923531541461471)
XLA Ops:
  0.6 93.6 %shard_map.112 = (f32[1,8]{1,0:T(1,128)}, f32[64,768]{1,0:T(8,128)}, bf16[2048,768]{1,0:T(8,128)(2,1)}) custom-call(bf16[8,1024]{1,0:T(8,128)(2,1)} %h_ref.1, s32[8,128]{1,0:T(8,128)} %bitcast.4, s32[8,128]{1,0:T(8,128)} %row_ref.1, s32[8]{0:T(128)} %count_ref.1, bf16[8,768]{1,0:T(8,128)(2,1)} %pos_ref.1, bf16[48,1024]{1,0:T(8,128)(2,1)} %bitcast.3, ...), custom_call_target="tpu_custom_call" | custom-call | flops 30000001024 | bytes 16777216 | tf_op jit(solution)/shard_map/pallas_call | solution.py:609
  94.3 4.5 %shard_map.113 = (f32[1,8]{1,0:T(1,128)}, f32[64,768]{1,0:T(8,128)}, bf16[2048,768]{1,0:T(8,128)(2,1)}) custom-call(f32[1,8]{1,0:T(1,128)} %get-tuple-element.9.loss_in, f32[64,768]{1,0:T(8,128)} %get-tuple-element.10.grad_in, bf16[2048,768]{1,0:T(8,128)(2,1)} %get-tuple-element.11.ren_in), custom_call_target="tpu_custom_call" | custom-call | tf_op jit(solution)/shard_map/pallas_call | solution.py:625

commit v3 on v2

--- a/solution.py
+++ b/solution.py
@@ -14,7 +14,6 @@
 D = 1024
 SCALE = 1.0 / (E * DIV)
 NX, NY, NZ = 4, 4, 8
-X_FIRST = (True, True, False, True, False, False)
 
 
 def iota(shape, dim):
@@ -38,8 +37,8 @@
     loss_ref, grad_ref, ren_hbm,
     wq, idx, slab, ren, local_sem,
     buf_a, buf_b, h_t, tab, tab_y, tab_j, tab_r,
-    pbuf, rows, norm, u_two, u_scale, ghat, gmat, zbuf, zrecv, zsum, zcol,
-    tt, tcore, tsum, r1, p1, r2, p2, r3, fin,
+    pbuf, rows, norm, u_two, u_scale, ghat, gother, posd, posd_in, gmat, zbuf, zrecv, zsum, zcol,
+    tt, r1, p1, r2, p2, r3, fin,
     ssem, rsem,
 ):
     g = lax.axis_index("group")
@@ -152,6 +151,16 @@
 
     loads[2].start()
 
+    await_bytes(ty_sem, tab_y.at[0:15])
+    tab_j[...] = jnp.swapaxes(tab_y[...].astype(F32), 0, 1).astype(BF16)
+    s, tj_sem = send_sem(tab_r.at[0:15]), recv_sem()
+    for o in range(NZ):
+        for k in range(2):
+            if o or k:
+                to = near(0, 0, o, k)
+                copy(tab_j.at[to[2] * 2 + to[3]], tab_r.at[z * 2 + c], to, s, tj_sem)
+    tab_r[z * 2 + c] = tab_j[z * 2 + c]
+
     loads[0].wait()
     q_own = jnp.dot(h_ref[...], wq[...], preferred_element_type=F32)
     rq_own = lax.rsqrt(jnp.mean(q_own * q_own, axis=1, keepdims=True) + EPS)
@@ -162,6 +171,10 @@
     pos_score = pos_dot * SCALE
     pos_exp = jnp.exp(pos_score)
     pos_dir = (pos - u_own * (pos_dot * (1.0 / E))) * (rq_own * SCALE)
+    for k in range(2):
+        posd[k] = pos_dir[:, k * 384:(k + 1) * 384]
+    s, posd_sem = send_sem(posd.at[0]), recv_sem()
+    copy(posd.at[1 - c], posd_in, near(0, 0, 0, 1), s, posd_sem)
 
     def along_x(o):
         return (o, 0, 0, 0)
@@ -211,16 +224,6 @@
         for o in range(1, 4):
             copy(ref, ref, near(*mid_axis[n](o)), s_mid[n], mid_sem[n][o - 1])
         to_near(n, 0)
-
-    await_bytes(ty_sem, tab_y.at[0:15])
-    tab_j[...] = jnp.swapaxes(tab_y[...].astype(F32), 0, 1).astype(BF16)
-    s, tj_sem = send_sem(tab_r.at[0:15]), recv_sem()
-    for o in range(NZ):
-        for k in range(2):
-            if o or k:
-                to = near(0, 0, o, k)
-                copy(tab_j.at[to[2] * 2 + to[3]], tab_r.at[z * 2 + c], to, s, tj_sem)
-    tab_r[z * 2 + c] = tab_j[z * 2 + c]
 
     await_bytes(px_sem, pbuf.at[0, 0, 0:3])
     s, pz_sem = send_sem(pbuf.at[0, 0:3]), recv_sem()
@@ -328,7 +331,10 @@
         gb = tn((e * rr).astype(BF16), r)
         u = two[0:256].astype(F32) + two[256:512].astype(F32)
         gb = gb - u * (jnp.sum(u * gb, axis=1, keepdims=True) * (1.0 / E))
-        ghat[pl.ds(pl.multiple_of(b * 256, 256), 256), :] = gb * u_scale[b][:, 0:1]
+        gb = gb * u_scale[b][:, 0:1]
+        at = pl.ds(pl.multiple_of(b * 256, 256), 256)
+        ghat[0, at, :] = gb[:, 0:384]
+        ghat[1, at, :] = gb[:, 384:768]
         return 0
 
     own_at = ((z * 2 + c) * 16 + x * 4 + y) * 8
@@ -386,21 +392,36 @@
         lax.fori_loop(lo, hi, step, 0)
 
     own = pl.ds(pl.multiple_of(own_at, 8), 8)
-
-    def rescale(k):
+    partner = pl.ds(pl.multiple_of(((z * 2 + 1 - c) * 16 + x * 4 + y) * 8, 8), 8)
+    g_sems = []
+
+    def terms_core(k):
         @pl.when(own_at // 1024 == k)
         def _():
-            z_here = zcol[own, :][:, 0:1]
-            ghat[own, :] = ghat[own, :] + pos_dir * (pos_exp - z_here)
+            for t in range(2):
+                ghat[t, own, :] = ghat[t, own, :] + posd[t] * pos_exp
+
+        span = pl.ds(k * 1024, 1024)
+        s, r = send_sem(gother.at[span]), recv_sem()
+        copy(ghat.at[1 - c, span], gother.at[span], near(0, 0, 0, 1), s, r)
+        g_sems.append(r)
+
+    def rescale(k):
+        await_bytes(g_sems[k], gother.at[pl.ds(k * 1024, 1024)])
+
+        @pl.when(own_at // 1024 == k)
+        def _():
+            ghat[c, own, :] = ghat[c, own, :] - posd[c] * zcol[own, :][:, 0:1]
+            ghat[c, partner, :] = ghat[c, partner, :] - posd_in[...] * zcol[partner, :][:, 0:1]
 
         def step(b, _):
             at = pl.ds(pl.multiple_of(b * 128, 128), 128)
-            gmat[at, :] = (ghat[at, :] / zcol[at, :][:, 0:1]).astype(BF16)
+            gmat[at, :] = ((ghat[c, at, :] + gother[at, :]) / zcol[at, :][:, 0:1]).astype(BF16)
             return 0
 
-        lax.fori_loop(k * 8, k * 8 + 8, step, 0)
-
-    unit_x = [jnp.int32(1), 1 - c, jnp.int32(0)]
+        lax.fori_loop(k * 8, k * 8 + 8, step, 0, unroll=4)
+
+    unit_x = [1, 1 - c, 0]
     first_at = [x * f + y * (1 - f) for f in unit_x]
     second_at = [y * f + x * (1 - f) for f in unit_x]
     quarter = [lax.rem(zl + 1 + n, 4) for n in range(4)]
@@ -411,75 +432,74 @@
         return jnp.dot(h_t[at, span], gmat[span, :], preferred_element_type=F32)
 
     def keep(n, val, more):
-        for t in range(6):
-            tile = val[:, t * 128:(t + 1) * 128].reshape(4, 4, 16, 128)
-            if X_FIRST[t]:
-                tt[n, t] = tt[n, t] + tile if more else tile
-            else:
-                for a in range(4):
-                    for b in range(4):
-                        part = tile[b, a]
-                        tt[n, t, a, b] = tt[n, t, a, b] + part if more else part
+        for u in range(3):
+            tile = val[:, u * 128:(u + 1) * 128].reshape(4, 4, 16, 128)
+            if u == 0:
+                tt[n, u] = tt[n, u] + tile if more else tile
+                continue
+            for i in range(4):
+                for j in range(4):
+                    a = i * unit_x[u] + j * (1 - unit_x[u])
+                    b = j * unit_x[u] + i * (1 - unit_x[u])
+                    part = tile[i, j]
+                    tt[n, u, a, b] = tt[n, u, a, b] + part if more else part
 
     lax.fori_loop(0, 4, score, 0, unroll=4)
     sums_core(0)
+    terms_core(0)
     lax.fori_loop(4, 6, score, 0, unroll=2)
     xy_0 = sums_xy(0)
     lax.fori_loop(6, 8, score, 0, unroll=2)
     sums_core(1)
+    terms_core(1)
     za_0 = sums_z(0, xy_0)
     loads[2].wait()
     await_bytes(pc_sem, pbuf.at[0])
-    encode(0, 2)
+    encode(0, 1)
     xy_1 = sums_xy(1)
-    encode(2, 5)
+    encode(1, 3)
     sums_done(0, za_0)
+    await_bytes(posd_sem, posd_in)
     rescale(0)
-    keep(0, product(0, 0), False)
     za_1 = sums_z(1, xy_1)
-    for n in range(1, 4):
+    for n in range(4):
         keep(n, product(n, 0), False)
-    encode(5, 8)
-    out_copy = pltpu.make_async_copy(ren, ren_hbm, local_sem.at[3])
-    out_copy.start()
+    encode(3, 4)
     sums_done(1, za_1)
     rescale(1)
 
     z_own = zcol[own, :][:, 0:1]
     loss = jnp.log(z_own) - pos_score
     loss_ref[...] = jnp.sum(jnp.where(sub == ln, loss, 0.0), axis=0, keepdims=True)[:, 0:8]
-    own_rows = ghat[own, :] / z_own
-    own_low = own_rows - own_rows.astype(BF16).astype(F32)
-    own_low = jnp.concatenate([own_low, jnp.zeros_like(own_low)], axis=0).astype(BF16)
-    h_pad = jnp.concatenate([h32, jnp.zeros_like(h32)], axis=0)
-    h_pad = jnp.concatenate(
-        [h_pad[:, n * 256:(n + 1) * 256] for n in range(4)], axis=0
-    ).astype(BF16)
-
-    s_tc, tc_sem = send_sem(tcore), [recv_sem() for _ in range(4)]
+    pair_rows = jnp.concatenate(
+        [(ghat[c, at, :] + gother[at, :]) / zcol[at, :][:, 0:1] for at in (own, partner)], axis=0
+    )
+    pair_low = (pair_rows - pair_rows.astype(BF16).astype(F32)).astype(BF16)
+    pair_h = []
+    for buf in bufs:
+        mine, its = buf[x, c, y, z].astype(F32), buf[x, 1 - c, y, z].astype(F32)
+        for at in (slice(0, 8), slice(8, 16)):
+            pair_h.append(jnp.concatenate([mine[at], its[at]], axis=0))
+
     s_r1, r1_sem = send_sem(r1), [recv_sem() for _ in range(4)]
     s_r2, r2_sem = send_sem(r2), [recv_sem() for _ in range(4)]
     s_r3, r3_sem = send_sem(r3), recv_sem()
-    hpt = h_pad.reshape(4, 16, 256)
 
     def produce(n):
         val = product(n, 1)
         mine = jnp.zeros((16, 256), F32)
         for t in range(4):
-            mine = jnp.where(quarter[n] == t, hpt[t].astype(F32), mine)
-        val = val + tn(mine.astype(BF16), own_low)
+            mine = jnp.where(quarter[n] == t, pair_h[t], mine)
+        val = val + tn(mine.astype(BF16), pair_low)
         keep(n, val, True)
-        copy(tt.at[n, pl.ds((1 - c) * 3, 3)], tcore.at[n], near(0, 0, 0, 1), s_tc, tc_sem[n])
 
     def step_first(n):
-        await_bytes(tc_sem[n], tcore.at[n])
         for u in range(3):
             f = unit_x[u]
-            tsum[n, u] = tt[n, c * 3 + u] + tcore[n, u]
             for o in range(1, 4):
                 to = lax.rem(first_at[u] + o, 4)
                 copy(
-                    tsum.at[n, u, to], r1.at[n, u, o - 1], near(o * f, o * (1 - f), 0, 0),
+                    tt.at[n, u, to], r1.at[n, u, o - 1], near(o * f, o * (1 - f), 0, 0),
                     s_r1, r1_sem[n],
                 )
 
@@ -487,7 +507,7 @@
         await_bytes(r1_sem[n], r1.at[n])
         for u in range(3):
             f = unit_x[u]
-            p1[n, u] = tsum[n, u, first_at[u]] + (r1[n, u, 0] + r1[n, u, 1] + r1[n, u, 2])
+            p1[n, u] = tt[n, u, first_at[u]] + (r1[n, u, 0] + r1[n, u, 1] + r1[n, u, 2])
             for o in range(1, 4):
                 to = lax.rem(second_at[u] + o, 4)
                 copy(
@@ -507,19 +527,20 @@
                 away = lax.rem(to - z + NZ, NZ)
                 copy(p2.at[n], r3.at[away - 1], (x, y, to, c), s_r3, r3_sem)
 
-    produce(0)
-    produce(1)
-    step_first(0)
-    produce(2)
-    step_first(1)
-    produce(3)
-    step_first(2)
+    for n in range(4):
+        produce(n)
+        step_first(n)
+    encode(4, 5)
     step_second(0)
-    step_first(3)
+    encode(5, 6)
     step_second(1)
     step_z(0)
+    encode(6, 7)
     step_second(2)
     step_z(1)
+    encode(7, 8)
+    out_copy = pltpu.make_async_copy(ren, ren_hbm, local_sem.at[3])
+    out_copy.start()
     step_second(3)
     step_z(2)
     step_z(3)
@@ -546,7 +567,7 @@
 
 
 def hand_over(loss_in, grad_in, ren_in, loss_out, grad_out, ren_out, held, sem):
-    parts = 4
+    parts = 2
     size = ren_in.shape[0] // parts
     ins, outs = [], []
     for n in range(parts):
@@ -564,8 +585,8 @@
         copy.wait()
 
 
-SENDS = 26
-RECVS = 45
+SENDS = 28
+RECVS = 44
 
 
 def local(
@@ -592,9 +613,9 @@
         V((16, 16, 128), BF16),
         V((2, 4, 4, 48, 512), BF16), V((8, 256, E), BF16), V((8, 2, 256, 128), F32),
         V((8, 512, E), BF16), V((8, 256, 128), F32),
-        V((2048, E), F32), V((2048, E), BF16),
+        V((2, 2048, 384), F32), V((2048, 384), F32), V((2, 8, 384), F32), V((8, 384), F32),
+        V((2048, 384), BF16),
         V((2, 8, 128), F32), V((2, 23, 8, 128), F32), V((2, 2, 8, 128), F32), V((2048, 128), F32),
-        V((4, 6, 4, 4, 16, 128), F32), V((4, 3, 4, 4, 16, 128), F32),
         V((4, 3, 4, 4, 16, 128), F32),
         V((4, 3, 3, 4, 16, 128), F32), V((4, 3, 4, 16, 128), F32),
         V((4, 3, 3, 16, 128), F32), V((4, 3, 16, 128), F32),
@@ -627,7 +648,7 @@
         out_shape=shapes,
         in_specs=[vmem, vmem, hbm],
         out_specs=(vmem, vmem, hbm),
-        scratch_shapes=[V((2048, E), BF16), pltpu.SemaphoreType.DMA((8,))],
+        scratch_shapes=[V((2048, E), BF16), pltpu.SemaphoreType.DMA((4,))],
         compiler_params=pltpu.CompilerParams(vmem_limit_bytes=62 * 2**20),
     )(*results)
     return losses.reshape(8), grad, renewed

time: 99.1 us -> 97.6 us (0.985)
  Pallas kernels: 98.1 us -> 96.6 us
    pallas_call x1, Pallas kernels: 93.6 us -> 91.9 us  [local(): pl.pallas_call(body, out_shape=shapes, in_specs=[vmem, vmem, vmem, smem,...]
where the time goes in v3:
time: 97.6 us; the launch traced here: 97.4 us
  Pallas kernels  96.6 us (99%)
    pallas_call x1, Pallas kernels, local(): pl.pallas_call(body, out_shape=shapes, in_specs=[vmem, vmem, vmem, smem,...  91.9 us
    pallas_call x1, Pallas kernels, local(): pl.pallas_call(hand_over, out_shape=shapes, in_specs=[vmem, vmem, hbm], o...  4.72 us

profile of v3, /device:TPU:1, one launch (start us, length us, event | category | flops | bytes accessed | tf_op | source)
XLA Modules:
  0.0 97.4 jit_solution(11802940758790132726)
XLA Ops:
  0.6 91.9 %shard_map.112 = (f32[1,8]{1,0:T(1,128)}, f32[64,768]{1,0:T(8,128)}, bf16[2048,768]{1,0:T(8,128)(2,1)}) custom-call(bf16[8,1024]{1,0:T(8,128)(2,1)} %h_ref.1, s32[8,128]{1,0:T(8,128)} %bitcast.4, s32[8,128]{1,0:T(8,128)} %row_ref.1, s32[8]{0:T(128)} %count_ref.1, bf16[8,768]{1,0:T(8,128)(2,1)} %pos_ref.1, bf16[48,1024]{1,0:T(8,128)(2,1)} %bitcast.3, ...), custom_call_target="tpu_custom_call" | custom-call | flops 30000001024 | bytes 16777216 | tf_op jit(solution)/shard_map/pallas_call | solution.py:630
  92.5 4.7 %shard_map.113 = (f32[1,8]{1,0:T(1,128)}, f32[64,768]{1,0:T(8,128)}, bf16[2048,768]{1,0:T(8,128)(2,1)}) custom-call(f32[1,8]{1,0:T(1,128)} %get-tuple-element.9.loss_in, f32[64,768]{1,0:T(8,128)} %get-tuple-element.10.grad_in, bf16[2048,768]{1,0:T(8,128)(2,1)} %get-tuple-element.11.ren_in), custom_call_target="tpu_custom_call" | custom-call | tf_op jit(solution)/shard_map/pallas_call | solution.py:646

commit v4 on v3

--- a/solution.py
+++ b/solution.py
@@ -151,16 +151,6 @@
 
     loads[2].start()
 
-    await_bytes(ty_sem, tab_y.at[0:15])
-    tab_j[...] = jnp.swapaxes(tab_y[...].astype(F32), 0, 1).astype(BF16)
-    s, tj_sem = send_sem(tab_r.at[0:15]), recv_sem()
-    for o in range(NZ):
-        for k in range(2):
-            if o or k:
-                to = near(0, 0, o, k)
-                copy(tab_j.at[to[2] * 2 + to[3]], tab_r.at[z * 2 + c], to, s, tj_sem)
-    tab_r[z * 2 + c] = tab_j[z * 2 + c]
-
     loads[0].wait()
     q_own = jnp.dot(h_ref[...], wq[...], preferred_element_type=F32)
     rq_own = lax.rsqrt(jnp.mean(q_own * q_own, axis=1, keepdims=True) + EPS)
@@ -224,6 +214,16 @@
         for o in range(1, 4):
             copy(ref, ref, near(*mid_axis[n](o)), s_mid[n], mid_sem[n][o - 1])
         to_near(n, 0)
+
+    await_bytes(ty_sem, tab_y.at[0:15])
+    tab_j[...] = jnp.swapaxes(tab_y[...].astype(F32), 0, 1).astype(BF16)
+    s, tj_sem = send_sem(tab_r.at[0:15]), recv_sem()
+    for o in range(NZ):
+        for k in range(2):
+            if o or k:
+                to = near(0, 0, o, k)
+                copy(tab_j.at[to[2] * 2 + to[3]], tab_r.at[z * 2 + c], to, s, tj_sem)
+    tab_r[z * 2 + c] = tab_j[z * 2 + c]
 
     await_bytes(px_sem, pbuf.at[0, 0, 0:3])
     s, pz_sem = send_sem(pbuf.at[0, 0:3]), recv_sem()
@@ -567,7 +567,7 @@
 
 
 def hand_over(loss_in, grad_in, ren_in, loss_out, grad_out, ren_out, held, sem):
-    parts = 2
+    parts = 4
     size = ren_in.shape[0] // parts
     ins, outs = [], []
     for n in range(parts):
@@ -648,7 +648,7 @@
         out_shape=shapes,
         in_specs=[vmem, vmem, hbm],
         out_specs=(vmem, vmem, hbm),
-        scratch_shapes=[V((2048, E), BF16), pltpu.SemaphoreType.DMA((4,))],
+        scratch_shapes=[V((2048, E), BF16), pltpu.SemaphoreType.DMA((8,))],
         compiler_params=pltpu.CompilerParams(vmem_limit_bytes=62 * 2**20),
     )(*results)
     return losses.reshape(8), grad, renewed

time: 97.6 us -> 95.4 us (0.977)
  Pallas kernels: 96.6 us -> 94.5 us
    pallas_call x1, Pallas kernels: 91.9 us -> 90 us  [local(): pl.pallas_call(body, out_shape=shapes, in_specs=[vmem, vmem, vmem, smem,...]
where the time goes in v4:
time: 95.4 us; the launch traced here: 95.3 us
  Pallas kernels  94.5 us (99%)
    pallas_call x1, Pallas kernels, local(): pl.pallas_call(body, out_shape=shapes, in_specs=[vmem, vmem, vmem, smem,...  90 us
    pallas_call x1, Pallas kernels, local(): pl.pallas_call(hand_over, out_shape=shapes, in_specs=[vmem, vmem, hbm], o...  4.47 us

profile of v4, /device:TPU:1, one launch (start us, length us, event | category | flops | bytes accessed | tf_op | source)
XLA Modules:
  0.0 95.3 jit_solution(16474278535986876432)
XLA Ops:
  0.6 90.0 %shard_map.112 = (f32[1,8]{1,0:T(1,128)}, f32[64,768]{1,0:T(8,128)}, bf16[2048,768]{1,0:T(8,128)(2,1)}) custom-call(bf16[8,1024]{1,0:T(8,128)(2,1)} %h_ref.1, s32[8,128]{1,0:T(8,128)} %bitcast.4, s32[8,128]{1,0:T(8,128)} %row_ref.1, s32[8]{0:T(128)} %count_ref.1, bf16[8,768]{1,0:T(8,128)(2,1)} %pos_ref.1, bf16[48,1024]{1,0:T(8,128)(2,1)} %bitcast.3, ...), custom_call_target="tpu_custom_call" | custom-call | flops 30000001024 | bytes 16777216 | tf_op jit(solution)/shard_map/pallas_call | solution.py:630
  90.6 4.5 %shard_map.113 = (f32[1,8]{1,0:T(1,128)}, f32[64,768]{1,0:T(8,128)}, bf16[2048,768]{1,0:T(8,128)(2,1)}) custom-call(f32[1,8]{1,0:T(1,128)} %get-tuple-element.9.loss_in, f32[64,768]{1,0:T(8,128)} %get-tuple-element.10.grad_in, bf16[2048,768]{1,0:T(8,128)(2,1)} %get-tuple-element.11.ren_in), custom_call_target="tpu_custom_call" | custom-call | tf_op jit(solution)/shard_map/pallas_call | solution.py:646
